TPU v7x, 128 devices: a whole 4x4x4 slice. The times are simulated.
128 devices in a mesh: row: 8 (over z, core), col: 16 (over y, x).
Axes of the slice: x: 4, y: 4, z: 4, core: 2. Of those that a mesh axis runs over, the one named last changes fastest.
Arguments:
- start: float32 [98304, 32], P(('row', 'col')), may hold values from -410 to 410
- self_weight: float32 [98304], P(('row', 'col')), may hold values from 1 to 3
- blocks: bfloat16 [8, 16, 128, 256, 256], P('row', 'col'), may hold values from -0.0625 to 0.0625
- slot_row: int32 [8, 16, 128], P('row', 'col'), may hold values from 0 to 47, as said below
- slot_col: int32 [8, 16, 128], P('row', 'col'), may hold values from 0 to 23
- slot_count: int32 [8, 16], P('row', 'col'), may hold values from 3 to 128, as said below
Outputs:
- basis: float32 [98304, 32], P(('row', 'col'))
Inputs may be any that keep to these rules, and one draw needn't show every extreme that they name: `slot_row`: slots that a grid position uses name distinct blocks with I < J. `slot_count`: some position of grid row 0 uses all 128 slots.
All inputs are finite; a program needn't handle non-finite values.
Results may differ from a plain program's by a relative error of at most 0.0021.
Values may be sent and summed in bfloat16 or wider, within the bound.
A program may use at most 128 MiB of HBM per device.

v0:
```python
import jax
import jax.numpy as jnp
from jax import lax
from jax.sharding import PartitionSpec as P

ITERS = 2


def shards(start, self_weight, blocks, slot_row, slot_col, slot_count):
    grid_rows = lax.axis_size("row")
    grid_cols = lax.axis_size("col")
    row_here = lax.axis_index("row")
    col_here = lax.axis_index("col")
    capacity = blocks.shape[2]
    block_side = blocks.shape[3]
    vec_count = start.shape[1]
    owned_blocks = start.shape[0] // block_side
    group_rows = owned_blocks * grid_cols
    group_cols = owned_blocks * grid_rows
    total_rows = start.shape[0] * grid_rows * grid_cols
    stored = blocks.reshape(capacity, block_side, block_side)
    rows_index = slot_row.reshape(capacity)
    cols_index = slot_col.reshape(capacity)
    live_slots = (jnp.arange(capacity) < slot_count.reshape(())).astype(jnp.float32)
    row_onehot = (rows_index[None, :] == jnp.arange(group_rows)[:, None]).astype(
        jnp.float32
    ) * live_slots[None, :]
    col_onehot = (cols_index[None, :] == jnp.arange(group_cols)[:, None]).astype(
        jnp.float32
    ) * live_slots[None, :]
    basis = start
    for iteration in range(ITERS):
        packed = basis.astype(jnp.bfloat16).reshape(owned_blocks, block_side * vec_count)
        gathered = lax.all_gather(packed, ("row", "col"), axis=0, tiled=True)
        row_group = lax.dynamic_slice_in_dim(gathered, row_here * group_rows, group_rows, 0)
        col_group = lax.dynamic_index_in_dim(
            gathered.reshape(grid_rows, grid_cols, owned_blocks, block_side * vec_count),
            col_here,
            1,
            keepdims=False,
        ).reshape(group_cols, block_side * vec_count)
        far_vectors = col_group[cols_index].reshape(capacity, block_side, vec_count)
        near_vectors = row_group[rows_index].reshape(capacity, block_side, vec_count)
        forward = jnp.einsum(
            "sab,sbk->sak", stored, far_vectors, preferred_element_type=jnp.float32
        ).reshape(capacity, block_side * vec_count)
        backward = jnp.einsum(
            "sab,sak->sbk", stored, near_vectors, preferred_element_type=jnp.float32
        ).reshape(capacity, block_side * vec_count)
        row_sums = lax.psum_scatter(
            jnp.dot(
                row_onehot,
                forward,
                precision=lax.Precision.HIGHEST,
                preferred_element_type=jnp.float32,
            ),
            "col",
            scatter_dimension=0,
            tiled=True,
        )
        col_sums = lax.psum_scatter(
            jnp.dot(
                col_onehot,
                backward,
                precision=lax.Precision.HIGHEST,
                preferred_element_type=jnp.float32,
            ),
            "row",
            scatter_dimension=0,
            tiled=True,
        )
        summed = row_sums + col_sums
        image = self_weight[:, None] * basis + summed.reshape(owned_blocks * block_side, vec_count)
        local_gram = jnp.dot(
            image.T, image, precision=lax.Precision.HIGHEST, preferred_element_type=jnp.float32
        )
        gram_matrix = lax.psum(local_gram, ("row", "col")) / total_rows
        factor = jnp.linalg.cholesky(gram_matrix)
        basis = jax.scipy.linalg.solve_triangular(factor, image.T, lower=True).T
    return basis


def solution(mesh):
    placed = (
        P(("row", "col"), None),
        P(("row", "col")),
        P("row", "col", None, None, None),
        P("row", "col", None),
        P("row", "col", None),
        P("row", "col"),
    )
    return jax.shard_map(
        shards, mesh=mesh, in_specs=placed, out_specs=P(("row", "col"), None), check_vma=False
    )
```

profile of v0, /device:TPU:1, one launch (start us, length us, event | category | flops | bytes accessed | tf_op | source)
XLA Modules:
  0.0 741.4 jit_solution(15894472085260505485)
XLA Ops:
  10.6 73.8 %all-gather.5.cloned.1.call-done = bf16[128,3,8192]{2,1,0:T(4,128)(2,1)} async-done(((bf16[1,3,8192]{2,1,0:T(4,128)(2,1)}), bf16[128,3,8192]{2,1,0:T(4,128)(2,1)}) %all-gather.5.cloned.1.call-update) | async-done | bytes 6291472 | tf_op jit(solution)/shard_map/all_gather | solution.py:34
  84.3 7.9 %copy.42 = bf16[128,3,8192]{2,0,1:T(8,128)(2,1)S(1)} copy(bf16[128,3,8192]{2,1,0:T(4,128)(2,1)} %all-gather.5.cloned.1.call-done) | data formatting | bytes 12582912 | tf_op jit(solution)/shard_map/all_gather | solution.py:34
  92.2 1.0 constant_dynamic-slice_fusion.3
  94.1 3.3 gather_fusion
  97.4 3.4 copy.44
  100.7 3.5 copy.45
  104.3 13.8 %reshape.187 = bf16[384,8192]{1,0:T(8,128)(2,1)} reshape(bf16[128,3,8192]{2,1,0:T(4,128)(2,1)} %all-gather.5.cloned.1.call-done) | data formatting | bytes 12582912
  118.0 1.2 constant_dynamic-slice_fusion.2
  119.2 1.9 gather_fusion.1
  121.1 2.5 copy.47
  123.6 3.9 copy.48
  127.5 10.7 %fusion.11 = f32[128,256,32]{1,2,0:T(8,128)} fusion(bf16[128,256,32]{1,2,0:T(8,128)(2,1)S(1)} %copy.48, bf16[1,1,128,256,256]{4,3,2,1,0:T(8,128)(2,1)} %param.11), kind=kOutput, calls=%fused_computation.13 | convolution fusion | flops 536870912 | bytes 23068672 | tf_op jit(solution)/shard_map/sab,sak->sbk/dot_general | solution.py:47
  138.2 6.0 copy.49
  144.2 6.7 fusion.39
  151.0 12.8 %fusion.8 = f32[128,256,32]{1,2,0:T(8,128)} fusion(bf16[128,256,32]{1,2,0:T(8,128)(2,1)S(1)} %copy-done.1, bf16[1,1,128,256,256]{4,3,2,1,0:T(8,128)(2,1)} %param.11), kind=kOutput, calls=%fused_computation.12 | convolution fusion | flops 536870912 | bytes 23068672 | tf_op jit(solution)/shard_map/sab,sbk->sak/dot_general | solution.py:44
  163.7 6.4 copy.46
  170.1 7.9 %fusion.27 = f32[48,8192]{1,0:T(8,128)} fusion(f32[128,8192]{0,1:T(8,128)} %bitcast.97, f32[128]{0:T(128)S(1)} %compare_convert_fusion, s32[128]{0:T(128)S(1)} %bitcast.105), kind=kOutput, calls=%fused_computation.29 | convolution fusion | flops 603992064 | bytes 5768192 | tf_op jit(solution)/shard_map/dot_general | solution.py:51
  180.7 27.3 %all-reduce.11.cloned.1.call-done = f32[24,8192]{1,0:T(8,128)} async-done(((f32[24,8192]{1,0:T(8,128)}), f32[24,8192]{1,0:T(8,128)}) %all-reduce.11.cloned.1.call-update) | async-done | bytes 786448
  208.0 91.9 %all-reduce.9.cloned.1.call-done = f32[48,8192]{1,0:T(8,128)} async-done(((f32[48,8192]{1,0:T(8,128)}), f32[48,8192]{1,0:T(8,128)}) %all-reduce.9.cloned.1.call-update) | async-done | bytes 1572880
  299.9 1.2 dynamic-slice_add_fusion.1
  301.3 1.0 fusion.23
  302.3 65.9 %psum.14 = f32[32,32]{0,1:T(8,128)S(1)} all-reduce(f32[32,32]{0,1:T(8,128)S(1)} %fusion.23), channel_id=1, replica_groups=mesh['row'=8,'col'=16] {'row','col'}, use_global_device_ids=true, to_apply=%region_2.3 | all-reduce | flops 1024 | bytes 8192 | tf_op jit(solution)/shard_map/psum | solution.py:77
  368.3 2.9 cholesky.44
  372.5 2.4 custom-call.6
  376.8 67.1 %all-gather.7.cloned.1.call-done = bf16[128,3,8192]{2,1,0:T(4,128)(2,1)} async-done(((bf16[1,3,8192]{2,1,0:T(4,128)(2,1)}), bf16[128,3,8192]{2,1,0:T(4,128)(2,1)}) %all-gather.7.cloned.1.call-update) | async-done | bytes 6291472 | tf_op jit(solution)/shard_map/all_gather | solution.py:34
  443.9 7.9 %copy.53 = bf16[128,3,8192]{2,0,1:T(8,128)(2,1)S(1)} copy(bf16[128,3,8192]{2,1,0:T(4,128)(2,1)} %all-gather.7.cloned.1.call-done) | data formatting | bytes 12582912 | tf_op jit(solution)/shard_map/all_gather | solution.py:34
  451.8 1.0 constant_dynamic-slice_fusion.1
  453.6 3.3 gather_fusion.2
  456.9 3.4 copy.55
  460.3 3.5 copy.56
  463.8 13.8 %reshape.189 = bf16[384,8192]{1,0:T(8,128)(2,1)} reshape(bf16[128,3,8192]{2,1,0:T(4,128)(2,1)} %all-gather.7.cloned.1.call-done) | data formatting | bytes 12582912
  477.6 1.2 constant_dynamic-slice_fusion
  478.7 1.9 gather_fusion.3
  480.6 2.5 copy.58
  483.1 3.9 copy.59
  487.0 10.7 %fusion.17 = f32[128,256,32]{1,2,0:T(8,128)} fusion(bf16[128,256,32]{1,2,0:T(8,128)(2,1)S(1)} %copy.59, bf16[1,1,128,256,256]{4,3,2,1,0:T(8,128)(2,1)} %param.11), kind=kOutput, calls=%fused_computation.15 | convolution fusion | flops 536870912 | bytes 23068672 | tf_op jit(solution)/shard_map/sab,sak->sbk/dot_general | solution.py:47
  497.7 6.0 copy.60
  503.7 6.7 fusion.37
  510.5 12.8 %fusion.14 = f32[128,256,32]{1,2,0:T(8,128)} fusion(bf16[128,256,32]{1,2,0:T(8,128)(2,1)S(1)} %copy-done, bf16[1,1,128,256,256]{4,3,2,1,0:T(8,128)(2,1)} %param.11), kind=kOutput, calls=%fused_computation.14 | convolution fusion | flops 536870912 | bytes 23068672 | tf_op jit(solution)/shard_map/sab,sbk->sak/dot_general | solution.py:44
  523.2 6.2 copy.57
  529.4 7.8 %fusion.25 = f32[48,8192]{1,0:T(8,128)} fusion(f32[128,8192]{0,1:T(8,128)} %bitcast.95, f32[128]{0:T(128)S(1)} %compare_convert_fusion, s32[128]{0:T(128)S(1)} %bitcast.106), kind=kOutput, calls=%fused_computation.27 | convolution fusion | flops 603992064 | bytes 5768192 | tf_op jit(solution)/shard_map/dot_general | solution.py:51
  537.2 30.2 %all-reduce.15.cloned.1.call-done = f32[24,8192]{1,0:T(8,128)} async-done(((f32[24,8192]{1,0:T(8,128)}), f32[24,8192]{1,0:T(8,128)}) %all-reduce.15.cloned.1.call-update) | async-done | bytes 786448
  567.5 91.3 %all-reduce.13.cloned.1.call-done = f32[48,8192]{1,0:T(8,128)} async-done(((f32[48,8192]{1,0:T(8,128)}), f32[48,8192]{1,0:T(8,128)}) %all-reduce.13.cloned.1.call-update) | async-done | bytes 1572880
  658.8 1.2 dynamic-slice_add_fusion
  660.6 65.9 %psum.15 = f32[32,32]{0,1:T(8,128)S(1)} all-reduce(f32[32,32]{0,1:T(8,128)S(1)} %fusion.24), channel_id=1, replica_groups=mesh['row'=8,'col'=16] {'row','col'}, use_global_device_ids=true, to_apply=%region_7.10 | all-reduce | flops 1024 | bytes 8192 | tf_op jit(solution)/shard_map/psum | solution.py:77
  726.6 2.9 cholesky.55
  730.9 2.4 custom-call.7
  733.3 1.0 convolution_bitcast_fusion
  (63 shorter events, 11.9 us)
Async XLA Ops:
  6.5 77.8 %all-gather.5.cloned.1.call-start = ((), (), s32[]{:S(2)}) async-start(), calls=%async_computation | async-start | bytes 8454144 | tf_op jit(solution)/shard_map/all_gather | solution.py:34
  8.5 199.5 %all-reduce.11.cloned.1.call-start = ((), (), s32[]{:S(2)}) async-start(), calls=%async_computation.3 | async-start | bytes 1572864
  138.2 6.0 copy-start.5
  144.2 6.8 copy-start.1
  150.9 149.0 %all-reduce.9.cloned.1.call-start = ((), (), s32[]{:S(2)}) async-start(), calls=%async_computation.2 | async-start | bytes 3145728
  163.7 6.4 copy-start.4
  170.1 8.0 %copy-start.2 = (f32[768,32]{0,1:T(8,128)S(1)}, f32[768,32]{0,1:T(8,128)}, u32[]{:S(2)}) copy-start(f32[768,32]{0,1:T(8,128)} %param.9) | copy-start | bytes 294916
  170.1 8.2 %copy-start.7 = (u32[128]{0:T(128)S(1)}, u32[128]{0:T(128)}, u32[]{:S(2)}) copy-start(u32[128]{0:T(128)} %constant.70) | copy-start | bytes 1540
  170.1 8.8 %copy-start.6 = (u32[128]{0:T(128)S(1)}, u32[128]{0:T(128)}, u32[]{:S(2)}) copy-start(u32[128]{0:T(128)} %constant.74) | copy-start | bytes 1540
  170.1 131.2 %copy-start.3 = (f32[768]{0:T(1024)S(1)}, f32[768]{0:T(1024)}, u32[]{:S(2)}) copy-start(f32[768]{0:T(1024)} %param.10) | copy-start | bytes 9220
  178.0 265.8 %all-gather.7.cloned.1.call-start = ((), (), s32[]{:S(2)}) async-start(), calls=%async_computation.1 | async-start | bytes 8454144 | tf_op jit(solution)/shard_map/all_gather | solution.py:34
  376.7 190.8 %all-reduce.15.cloned.1.call-start = ((), (), s32[]{:S(2)}) async-start(), calls=%async_computation.5 | async-start | bytes 1572864
  503.7 6.8 copy-start
  510.4 148.4 %all-reduce.13.cloned.1.call-start = ((), (), s32[]{:S(2)}) async-start(), calls=%async_computation.4 | async-start | bytes 3145728
Sparse Core Ops, SparseCore 0:
  10.5 73.7 all-gather.4
  151.0 56.9 all-reduce.10
  211.7 88.1 all-reduce.8
  376.8 66.9 all-gather.6
  510.5 56.8 all-reduce.14
  570.6 88.1 all-reduce.12
where the time goes:
time: 749 us; the launch traced here: 741 us
  waiting for transfers between devices  382 us (51%)
  blocking collectives  132 us (18%)
  local copies, waits for them, and re-layouts  115 us (15%)
  matrix products  78.9 us (11%)
  other arithmetic  18.1 us (2%)
  between operations  15.9 us (2%)
    unnamed x10, waiting for transfers between devices  241 us
    all_gather x2, waiting for transfers between devices, shards(): gathered = lax.all_gather(packed, ('row', 'col'), axis=0, tiled=True)  141 us
    psum x2, blocking collectives, shards(): gram_matrix = lax.psum(local_gram, ('row', 'col')) / total_rows  132 us
    unnamed x23, local copies, waits for them, and re-layouts  30.7 us
    dot_general x2, matrix products, shards(): jnp.einsum('sab,sbk->sak', stored, far_vectors, preferred_element_type=jn...  25.5 us
    dot_general x2, matrix products, shards(): jnp.einsum('sab,sak->sbk', stored, near_vectors, preferred_element_type=j...  21.5 us
    all_gather x2, local copies, waits for them, and re-layouts, shards(): gathered = lax.all_gather(packed, ('row', 'col'), axis=0, tiled=True)  15.8 us
    dot_general x2, matrix products, shards(): jnp.dot(row_onehot, forward, precision=lax.Precision.HIGHEST, preferred_e...  15.7 us
  transfers between devices with their start and end apart: 6, of which 6 were waited for; matrix products, arithmetic and copies ran while one was open for 8% of the time, Pallas kernels for 0%

commit v1 on v0

v1 whole, which is shorter than its diff:
```python
import functools

import jax
import jax.numpy as jnp
from jax import lax
from jax.experimental import pallas as pl
from jax.experimental.pallas import tpu as pltpu
from jax.sharding import PartitionSpec as P

ITERS = 2
MESH = pl.DeviceIdType.MESH
NT = (((1,), (1,)), ((), ()))
NN = (((1,), (0,)), ((), ()))
HIGH = lax.Precision.HIGHEST
F32 = jnp.float32
BF16 = jnp.bfloat16
UNROLL = 32
CHUNKS = 16


def sort_slots(keys, partner, spare):
    n = keys.shape[1]
    lane = lax.broadcasted_iota(jnp.int32, (n, n), 1)
    slot = lax.broadcasted_iota(jnp.int32, (n, n), 0)

    def down(row):
        return jnp.broadcast_to(row, (n, n)).T

    def total(mask, value):
        return jnp.sum(jnp.where(mask, value, 0), axis=0, keepdims=True)

    key_down = down(keys)
    key_across = jnp.broadcast_to(keys, (n, n))
    ahead = (key_down < key_across) | ((key_down == key_across) & (slot < lane))
    rank = total(ahead, 1)
    placed = down(rank) == lane
    order = total(placed, slot)
    other = total(placed, down(partner))
    ordered = total(placed, key_down)
    first_lane = lax.broadcasted_iota(jnp.int32, (1, n), 1)
    before = pltpu.roll(ordered, 1, 1)
    keep = jnp.where((first_lane > 0) & (before == ordered), 1, 0)
    last = total(key_down <= lane, 1) - 1
    last = jnp.where(total(key_down == lane, 1) > 0, last, spare)
    return order, other, keep, last


def inverse_factor(gram):
    k = gram.shape[0]
    row = lax.broadcasted_iota(jnp.int32, (k, 2 * k), 0)
    eye = (lax.broadcasted_iota(jnp.int32, (k, k), 0) == lax.broadcasted_iota(jnp.int32, (k, k), 1)).astype(F32)
    work = jnp.concatenate([gram, eye], axis=1)
    for j in range(k):
        scale = lax.rsqrt(work[j : j + 1, j : j + 1])
        pivot = work[j : j + 1, :] * scale
        column = work[:, j : j + 1] * scale
        work = jnp.where(row > j, work - column * pivot, jnp.where(row == j, pivot, work))
    return work[:, k:]


def kernel(
    grid_rows, grid_cols, total_rows,
    start_ref, weight_ref, blocks_ref, slot_row_ref, slot_col_ref, count_ref, out_ref,
    start_v, held, turned, index_v, index_s, row_vecs, col_vecs, sums, row_out, col_out,
    row_in, col_in, gram_row, gram_col,
    start_sem, block_sem, index_sem,
    row_vec_send, row_vec_recv, col_vec_send, col_vec_recv,
    row_out_send, row_out_recv, col_out_send, col_out_recv,
    gram_row_send, gram_row_recv, gram_col_send, gram_col_recv,
):
    r = lax.axis_index("row")
    c = lax.axis_index("col")
    slots, side, _ = held.shape
    owned = row_in.shape[2]
    k = start_v.shape[0]
    group_rows = owned * grid_cols
    group_cols = owned * grid_rows
    per_chunk = slots // CHUNKS

    def row_peer(n):
        return lax.rem(r + n, grid_rows)

    def col_peer(n):
        return lax.rem(c + n, grid_cols)

    start_copy = pltpu.make_async_copy(start_ref, start_v, start_sem)
    start_copy.start()
    block_copies = []
    for n in range(CHUNKS):
        part = pl.ds(n * per_chunk, per_chunk)
        block_copies.append(pltpu.make_async_copy(blocks_ref.at[part], held.at[part], block_sem.at[n]))
        block_copies[-1].start()

    barrier = pltpu.get_barrier_semaphore()
    for n in range(1, grid_rows):
        pl.semaphore_signal(barrier, inc=1, device_id=(row_peer(n), c), device_id_type=MESH)
    for n in range(1, grid_cols):
        pl.semaphore_signal(barrier, inc=1, device_id=(r, col_peer(n)), device_id_type=MESH)

    lane = lax.broadcasted_iota(jnp.int32, (1, slots), 1)
    live = lane < count_ref[0, 0]
    slot_row = slot_row_ref[0]
    slot_col = slot_col_ref[0]
    for base, (keys, partner) in enumerate(
        ((jnp.where(live, slot_row, group_rows), slot_col), (jnp.where(live, slot_col, group_cols), slot_row))
    ):
        for n, found in enumerate(sort_slots(keys, partner, slots)):
            index_v[base * 4 + n : base * 4 + n + 1, :] = found
    index_copy = pltpu.make_async_copy(index_v, index_s, index_sem)
    index_copy.start()

    zeros = jnp.zeros((k, side), F32)
    sums[0, slots] = zeros
    sums[1, slots] = zeros

    start_copy.wait()
    basis = start_v[...]

    def share(it, basis):
        copies = []
        for b in range(owned):
            rounded = basis[:, b * side : (b + 1) * side].astype(BF16)
            row_vecs[it, c, b] = rounded
            col_vecs[it, r, b] = rounded
        if it == 0:
            pl.semaphore_wait(barrier, grid_rows + grid_cols - 2)
        for n in range(1, grid_rows):
            copies.append(
                pltpu.make_async_remote_copy(
                    col_vecs.at[it, r], col_vecs.at[it, r], col_vec_send.at[it, n], col_vec_recv.at[it, n],
                    device_id=(row_peer(n), c), device_id_type=MESH,
                )
            )
        for n in range(1, grid_cols):
            copies.append(
                pltpu.make_async_remote_copy(
                    row_vecs.at[it, c], row_vecs.at[it, c], row_vec_send.at[it, n], row_vec_recv.at[it, n],
                    device_id=(r, col_peer(n)), device_id_type=MESH,
                )
            )
        for copy in copies:
            copy.start()
        return copies[: grid_rows - 1], copies[grid_rows - 1 :]

    def multiply(which, matrices, vectors, it, parts):
        def some(g, running):
            for u in range(UNROLL):
                s = g * UNROLL + u
                matrix = matrices[index_s[which * 4, s]]
                q = index_s[which * 4 + 1, s]
                vector = vectors[it, q // owned, q % owned]
                product = lax.dot_general(vector, matrix, NN, preferred_element_type=F32)
                running = running * index_s[which * 4 + 2, s].astype(F32) + product
                sums[which, s] = running
            return running

        lax.fori_loop(0, slots // UNROLL, some, zeros)

    def spread(it, which, size, here, staged, landed, send, recv, place):
        copies = []
        for n in range(1, size):
            to = lax.rem(here + n, size)
            for b in range(owned):
                staged[it, to, b] = sums[which, index_s[which * 4 + 3, to * owned + b]].astype(BF16)
            copies.append(
                pltpu.make_async_remote_copy(
                    staged.at[it, to], landed.at[it, here], send.at[it, n], recv.at[it, n],
                    device_id=place(to), device_id_type=MESH,
                )
            )
            copies[-1].start()
        return copies

    def reduce_gram(it, part, landed, size, here, send, recv, place):
        landed[it, here] = part
        copies = []
        for n in range(1, size):
            to = lax.rem(here + n, size)
            copies.append(
                pltpu.make_async_remote_copy(
                    landed.at[it, here], landed.at[it, here], send.at[it, n], recv.at[it, n],
                    device_id=place(to), device_id_type=MESH,
                )
            )
            copies[-1].start()
        for copy in copies:
            copy.wait()
        total = landed[it, 0]
        for n in range(1, size):
            total = total + landed[it, n]
        return total

    for it in range(ITERS):
        col_copies, row_copies = share(it, basis)
        if it == 0:
            index_copy.wait()
            for n in range(CHUNKS):
                block_copies[n].wait()

                def turn(m, _, n=n):
                    turned[n * per_chunk + m] = held[n * per_chunk + m].T
                    return 0

                lax.fori_loop(0, per_chunk, turn, 0, unroll=True)
        for copy in col_copies:
            copy.wait()
        multiply(0, turned, col_vecs, it, None)
        row_moves = spread(
            it, 0, grid_cols, c, row_out, row_in, row_out_send, row_out_recv, lambda to: (r, to)
        )
        for copy in row_copies:
            copy.wait()
        multiply(1, held, row_vecs, it, None)
        col_moves = spread(
            it, 1, grid_rows, r, col_out, col_in, col_out_send, col_out_recv, lambda to: (to, c)
        )
        image = []
        for b in range(owned):
            part = basis[:, b * side : (b + 1) * side]
            weight = weight_ref[pl.ds(b * side, side)].reshape(1, side)
            image.append(
                part * weight + sums[0, index_s[3, c * owned + b]] + sums[1, index_s[7, r * owned + b]]
            )
        for copy in row_moves:
            copy.wait()
        for n in range(1, grid_cols):
            at = col_peer(n)
            for b in range(owned):
                image[b] = image[b] + row_in[it, at, b].astype(F32)
        for copy in col_moves:
            copy.wait()
        for n in range(1, grid_rows):
            at = row_peer(n)
            for b in range(owned):
                image[b] = image[b] + col_in[it, at, b].astype(F32)
        image = jnp.concatenate(image, axis=1)
        gram = lax.dot_general(image, image, NT, precision=HIGH, preferred_element_type=F32)
        packed = jnp.concatenate([gram[n * 8 : n * 8 + 8] for n in range(k // 8)], axis=1)
        packed = reduce_gram(
            it, packed, gram_row, grid_rows, r, gram_row_send, gram_row_recv, lambda to: (to, c)
        )
        packed = reduce_gram(
            it, packed, gram_col, grid_cols, c, gram_col_send, gram_col_recv, lambda to: (r, to)
        )
        gram = jnp.concatenate([packed[:, n * k : n * k + k] for n in range(k // 8)], axis=0)
        inverse = inverse_factor(gram * (1.0 / total_rows))
        basis = lax.dot_general(inverse, image, NN, precision=HIGH, preferred_element_type=F32)
    out_ref[...] = basis


def solution(mesh):
    grid_rows, grid_cols = mesh.shape["row"], mesh.shape["col"]

    def shards(start, self_weight, blocks, slot_row, slot_col, slot_count):
        rows, k = start.shape
        slots, side = blocks.shape[2], blocks.shape[3]
        owned = rows // side
        group_rows, group_cols = owned * grid_cols, owned * grid_rows
        total_rows = rows * grid_rows * grid_cols
        any_space = pl.BlockSpec(memory_space=pl.ANY)
        vmem = pl.BlockSpec(memory_space=pltpu.VMEM)
        dma = pltpu.SemaphoreType.DMA
        turned = pl.pallas_call(
            functools.partial(kernel, grid_rows, grid_cols, total_rows),
            out_shape=jax.ShapeDtypeStruct((k, rows), F32),
            in_specs=[any_space, vmem, any_space, vmem, vmem, pl.BlockSpec(memory_space=pltpu.SMEM)],
            out_specs=vmem,
            scratch_shapes=[
                pltpu.VMEM((k, rows), F32),
                pltpu.VMEM((slots, side, side), BF16),
                pltpu.VMEM((slots, side, side), BF16),
                pltpu.VMEM((8, slots), jnp.int32),
                pltpu.SMEM((8, slots), jnp.int32),
                pltpu.VMEM((ITERS, grid_cols, owned, k, side), BF16),
                pltpu.VMEM((ITERS, grid_rows, owned, k, side), BF16),
                pltpu.VMEM((2, slots + 1, k, side), F32),
                pltpu.VMEM((ITERS, grid_cols, owned, k, side), BF16),
                pltpu.VMEM((ITERS, grid_rows, owned, k, side), BF16),
                pltpu.VMEM((ITERS, grid_cols, owned, k, side), BF16),
                pltpu.VMEM((ITERS, grid_rows, owned, k, side), BF16),
                pltpu.VMEM((ITERS, grid_rows, 8, k * k // 8), F32),
                pltpu.VMEM((ITERS, grid_cols, 8, k * k // 8), F32),
                dma,
                dma((CHUNKS,)),
                dma,
            ]
            + [dma((ITERS, n)) for n in (grid_cols, grid_cols, grid_rows, grid_rows)] * 2
            + [dma((ITERS, n)) for n in (grid_rows, grid_rows, grid_cols, grid_cols)],
            compiler_params=pltpu.CompilerParams(
                collective_id=0, has_side_effects=True, vmem_limit_bytes=60 * 2**20
            ),
        )(
            start.T,
            self_weight,
            blocks.reshape(slots, side, side),
            slot_row.reshape(1, 1, slots),
            slot_col.reshape(1, 1, slots),
            slot_count,
        )
        return turned.T

    placed = (
        P(("row", "col"), None),
        P(("row", "col")),
        P("row", "col", None, None, None),
        P("row", "col", None),
        P("row", "col", None),
        P("row", "col"),
    )
    return jax.shard_map(
        shards, mesh=mesh, in_specs=placed, out_specs=P(("row", "col"), None), check_vma=False
    )
```

time: 749 us -> 86.2 us (0.12)
  waiting for transfers between devices: 382 us -> 0 us
  blocking collectives: 132 us -> 0 us
  local copies, waits for them, and re-layouts: 115 us -> 1.54 us
  Pallas kernels: 0 us -> 83.8 us
  matrix products: 78.9 us -> 0 us
  other arithmetic: 18.1 us -> 0 us
  between operations: 15.9 us -> 0.66 us
    unnamed x10 -> x0, waiting for transfers between devices: 241 us -> none
    all_gather x2 -> x0, waiting for transfers between devices: 141 us -> none  [shards(): gathered = lax.all_gather(packed, ('row', 'col'), axis=0, tiled=True)]
    psum x2 -> x0, blocking collectives: 132 us -> none  [shards(): gram_matrix = lax.psum(local_gram, ('row', 'col')) / total_rows]
    pallas_call x0 -> x1, Pallas kernels: none -> 83.8 us  [shards(): pl.pallas_call(functools.partial(kernel, grid_rows, grid_cols, total_rows...]
    dot_general x10 -> x0, matrix products: 77.3 us -> none  [the longest x2 25.5 us: shards(): jnp.einsum('sab,sbk->sak', stored, far_vectors, preferred_element_type=jn...]
    unnamed x23 -> x1, local copies, waits for them, and re-layouts: 30.7 us -> 1.54 us
    dot_general x4 -> x0, local copies, waits for them, and re-layouts: 24.4 us -> none  [the longest x2 12.5 us: shards(): jnp.einsum('sab,sbk->sak', stored, far_vectors, preferred_element_type=jn...]
    gather x8 -> x0, local copies, waits for them, and re-layouts: 21.9 us -> none  [the longest x4 13.3 us: shards(): far_vectors = col_group[cols_index].reshape(capacity, block_side, vec_count)]
  transfers between devices with their start and end apart: 6 -> 0, of which waited for: 6 -> 0; matrix products, arithmetic and copies ran while one was open for 8% -> 0% of each run, Pallas kernels for 0% -> 0%
where the time goes in v1:
time: 86.2 us; the launch traced here: 86 us
  Pallas kernels  83.8 us (97%)
  local copies, waits for them, and re-layouts  1.54 us (2%)
    pallas_call x1, Pallas kernels, shards(): pl.pallas_call(functools.partial(kernel, grid_rows, grid_cols, total_rows...  83.8 us

profile of v1, /device:TPU:1, one launch (start us, length us, event | category | flops | bytes accessed | tf_op | source)
XLA Modules:
  0.0 86.0 jit_solution(15148637491687358279)
XLA Ops:
  0.7 83.8 %shard_map.64 = f32[32,768]{1,0:T(8,128)} custom-call(f32[32,768]{1,0:T(8,128)} %bitcast.5, f32[768]{0:T(1024)} %weight_ref.1, bf16[128,256,256]{2,1,0:T(8,128)(2,1)} %bitcast.3, s32[1,1,128]{2,1,0:T(1,128)} %slot_row_ref.1, s32[1,1,128]{2,1,0:T(1,128)} %slot_col_ref.1, s32[1,1]{1,0:T(1,128)S(6)} %copy.8.count_ref), custom_call_target="tpu_custom_call" | custom-call | tf_op jit(solution)/shard_map/pallas_call | solution.py:263
  84.4 1.5 %copy.9 = f32[768,32]{0,1:T(8,128)} copy(f32[768,32]{0,1:T(8,128)} %bitcast.4) | data formatting | bytes 196608

commit v2 on v1

--- a/solution.py
+++ b/solution.py
@@ -89,7 +89,6 @@
     for n in range(CHUNKS):
         part = pl.ds(n * per_chunk, per_chunk)
         block_copies.append(pltpu.make_async_copy(blocks_ref.at[part], held.at[part], block_sem.at[n]))
-        block_copies[-1].start()
 
     barrier = pltpu.get_barrier_semaphore()
     for n in range(1, grid_rows):
@@ -114,27 +113,27 @@
     sums[1, slots] = zeros
 
     start_copy.wait()
-    basis = start_v[...]
-
-    def share(it, basis):
+    image = start_v[...]
+
+    def share(it, vectors):
         copies = []
         for b in range(owned):
-            rounded = basis[:, b * side : (b + 1) * side].astype(BF16)
-            row_vecs[it, c, b] = rounded
-            col_vecs[it, r, b] = rounded
+            rounded = vectors[:, b * side : (b + 1) * side].astype(BF16)
+            row_vecs[it][c, b] = rounded
+            col_vecs[it][r, b] = rounded
         if it == 0:
             pl.semaphore_wait(barrier, grid_rows + grid_cols - 2)
         for n in range(1, grid_rows):
             copies.append(
                 pltpu.make_async_remote_copy(
-                    col_vecs.at[it, r], col_vecs.at[it, r], col_vec_send.at[it, n], col_vec_recv.at[it, n],
+                    col_vecs[it].at[r], col_vecs[it].at[r], col_vec_send.at[it, n], col_vec_recv.at[it, n],
                     device_id=(row_peer(n), c), device_id_type=MESH,
                 )
             )
         for n in range(1, grid_cols):
             copies.append(
                 pltpu.make_async_remote_copy(
-                    row_vecs.at[it, c], row_vecs.at[it, c], row_vec_send.at[it, n], row_vec_recv.at[it, n],
+                    row_vecs[it].at[c], row_vecs[it].at[c], row_vec_send.at[it, n], row_vec_recv.at[it, n],
                     device_id=(r, col_peer(n)), device_id_type=MESH,
                 )
             )
@@ -142,13 +141,13 @@
             copy.start()
         return copies[: grid_rows - 1], copies[grid_rows - 1 :]
 
-    def multiply(which, matrices, vectors, it, parts):
+    def multiply(which, matrices, vectors, it):
         def some(g, running):
             for u in range(UNROLL):
                 s = g * UNROLL + u
                 matrix = matrices[index_s[which * 4, s]]
                 q = index_s[which * 4 + 1, s]
-                vector = vectors[it, q // owned, q % owned]
+                vector = vectors[it][q // owned, q % owned]
                 product = lax.dot_general(vector, matrix, NN, preferred_element_type=F32)
                 running = running * index_s[which * 4 + 2, s].astype(F32) + product
                 sums[which, s] = running
@@ -171,18 +170,20 @@
             copies[-1].start()
         return copies
 
-    def reduce_gram(it, part, landed, size, here, send, recv, place):
+    def send_gram(it, part, landed, size, here, send, recv, place):
         landed[it, here] = part
         copies = []
         for n in range(1, size):
-            to = lax.rem(here + n, size)
             copies.append(
                 pltpu.make_async_remote_copy(
                     landed.at[it, here], landed.at[it, here], send.at[it, n], recv.at[it, n],
-                    device_id=place(to), device_id_type=MESH,
+                    device_id=place(lax.rem(here + n, size)), device_id_type=MESH,
                 )
             )
             copies[-1].start()
+        return copies
+
+    def add_gram(it, copies, landed, size):
         for copy in copies:
             copy.wait()
         total = landed[it, 0]
@@ -190,8 +191,30 @@
             total = total + landed[it, n]
         return total
 
+    def gram_begin(it, image):
+        gram = lax.dot_general(image, image, NT, precision=HIGH, preferred_element_type=F32)
+        packed = jnp.concatenate([gram[n * 8 : n * 8 + 8] for n in range(k // 8)], axis=1)
+        return send_gram(it, packed, gram_row, grid_rows, r, gram_row_send, gram_row_recv, lambda to: (to, c))
+
+    def gram_middle(it, copies):
+        packed = add_gram(it, copies, gram_row, grid_rows)
+        return send_gram(it, packed, gram_col, grid_cols, c, gram_col_send, gram_col_recv, lambda to: (r, to))
+
+    def gram_end(it, copies):
+        packed = add_gram(it, copies, gram_col, grid_cols)
+        gram = jnp.concatenate([packed[:, n * k : n * k + k] for n in range(k // 8)], axis=0)
+        return inverse_factor(gram * (1.0 / total_rows))
+
+    def normalise(inverse, image):
+        return lax.dot_general(inverse, image, NN, precision=HIGH, preferred_element_type=F32)
+
     for it in range(ITERS):
-        col_copies, row_copies = share(it, basis)
+        col_copies, row_copies = share(it, image)
+        if it == 0:
+            for copy in block_copies:
+                copy.start()
+        if it > 0:
+            gram_copies = gram_begin(it - 1, image)
         if it == 0:
             index_copy.wait()
             for n in range(CHUNKS):
@@ -204,48 +227,45 @@
                 lax.fori_loop(0, per_chunk, turn, 0, unroll=True)
         for copy in col_copies:
             copy.wait()
-        multiply(0, turned, col_vecs, it, None)
+        if it > 0:
+            gram_copies = gram_middle(it - 1, gram_copies)
+        multiply(0, turned, col_vecs, it)
         row_moves = spread(
             it, 0, grid_cols, c, row_out, row_in, row_out_send, row_out_recv, lambda to: (r, to)
         )
         for copy in row_copies:
             copy.wait()
-        multiply(1, held, row_vecs, it, None)
+        multiply(1, held, row_vecs, it)
         col_moves = spread(
             it, 1, grid_rows, r, col_out, col_in, col_out_send, col_out_recv, lambda to: (to, c)
         )
-        image = []
+        parts = []
         for b in range(owned):
-            part = basis[:, b * side : (b + 1) * side]
+            part = image[:, b * side : (b + 1) * side]
             weight = weight_ref[pl.ds(b * side, side)].reshape(1, side)
-            image.append(
+            parts.append(
                 part * weight + sums[0, index_s[3, c * owned + b]] + sums[1, index_s[7, r * owned + b]]
             )
+        if it > 0:
+            inverse = gram_end(it - 1, gram_copies)
+        for copy in col_moves:
+            copy.wait()
+        for n in range(1, grid_rows):
+            at = row_peer(n)
+            for b in range(owned):
+                parts[b] = parts[b] + col_in[it, at, b].astype(F32)
         for copy in row_moves:
             copy.wait()
         for n in range(1, grid_cols):
             at = col_peer(n)
             for b in range(owned):
-                image[b] = image[b] + row_in[it, at, b].astype(F32)
-        for copy in col_moves:
-            copy.wait()
-        for n in range(1, grid_rows):
-            at = row_peer(n)
-            for b in range(owned):
-                image[b] = image[b] + col_in[it, at, b].astype(F32)
-        image = jnp.concatenate(image, axis=1)
-        gram = lax.dot_general(image, image, NT, precision=HIGH, preferred_element_type=F32)
-        packed = jnp.concatenate([gram[n * 8 : n * 8 + 8] for n in range(k // 8)], axis=1)
-        packed = reduce_gram(
-            it, packed, gram_row, grid_rows, r, gram_row_send, gram_row_recv, lambda to: (to, c)
-        )
-        packed = reduce_gram(
-            it, packed, gram_col, grid_cols, c, gram_col_send, gram_col_recv, lambda to: (r, to)
-        )
-        gram = jnp.concatenate([packed[:, n * k : n * k + k] for n in range(k // 8)], axis=0)
-        inverse = inverse_factor(gram * (1.0 / total_rows))
-        basis = lax.dot_general(inverse, image, NN, precision=HIGH, preferred_element_type=F32)
-    out_ref[...] = basis
+                parts[b] = parts[b] + row_in[it, at, b].astype(F32)
+        image = jnp.concatenate(parts, axis=1)
+        if it > 0:
+            image = normalise(inverse, image)
+    last = ITERS - 1
+    inverse = gram_end(last, gram_middle(last, gram_begin(last, image)))
+    out_ref[...] = normalise(inverse, image)
 
 
 def solution(mesh):
@@ -271,8 +291,8 @@
                 pltpu.VMEM((slots, side, side), BF16),
                 pltpu.VMEM((8, slots), jnp.int32),
                 pltpu.SMEM((8, slots), jnp.int32),
-                pltpu.VMEM((ITERS, grid_cols, owned, k, side), BF16),
-                pltpu.VMEM((ITERS, grid_rows, owned, k, side), BF16),
+                [pltpu.VMEM((grid_cols, owned, k, side), BF16)] * ITERS,
+                [pltpu.VMEM((grid_rows, owned, k, side), BF16)] * ITERS,
                 pltpu.VMEM((2, slots + 1, k, side), F32),
                 pltpu.VMEM((ITERS, grid_cols, owned, k, side), BF16),
                 pltpu.VMEM((ITERS, grid_rows, owned, k, side), BF16),

time: 86.2 us -> 72.1 us (0.84)
  Pallas kernels: 83.8 us -> 69.7 us
    pallas_call x1, Pallas kernels: 83.8 us -> 69.7 us  [shards(): pl.pallas_call(functools.partial(kernel, grid_rows, grid_cols, total_rows...]
where the time goes in v2:
time: 72.1 us; the launch traced here: 71.9 us
  Pallas kernels  69.7 us (97%)
  local copies, waits for them, and re-layouts  1.54 us (2%)
    pallas_call x1, Pallas kernels, shards(): pl.pallas_call(functools.partial(kernel, grid_rows, grid_cols, total_rows...  69.7 us
    unnamed x1, local copies, waits for them, and re-layouts  1.54 us

profile of v2, /device:TPU:1, one launch (start us, length us, event | category | flops | bytes accessed | tf_op | source)
XLA Modules:
  0.0 71.9 jit_solution(5095278729059332621)
XLA Ops:
  0.7 69.7 %shard_map.64 = f32[32,768]{1,0:T(8,128)} custom-call(f32[32,768]{1,0:T(8,128)} %bitcast.5, f32[768]{0:T(1024)} %weight_ref.1, bf16[128,256,256]{2,1,0:T(8,128)(2,1)} %bitcast.3, s32[1,1,128]{2,1,0:T(1,128)} %slot_row_ref.1, s32[1,1,128]{2,1,0:T(1,128)} %slot_col_ref.1, s32[1,1]{1,0:T(1,128)S(6)} %copy.8.count_ref), custom_call_target="tpu_custom_call" | custom-call | tf_op jit(solution)/shard_map/pallas_call | solution.py:283
  70.4 1.5 %copy.9 = f32[768,32]{0,1:T(8,128)} copy(f32[768,32]{0,1:T(8,128)} %bitcast.4) | data formatting | bytes 196608

commit v3 on v2

--- a/solution.py
+++ b/solution.py
@@ -15,7 +15,10 @@
 F32 = jnp.float32
 BF16 = jnp.bfloat16
 UNROLL = 32
+HOPS = (2, 3, 1)
+Y_FIRST = ((1, 1), (1, 2), (1, 3), (2, 3), (3, 3))
 CHUNKS = 16
+EARLY_CHUNKS = 8
 
 
 def sort_slots(keys, partner, spare):
@@ -83,6 +86,15 @@
     def col_peer(n):
         return lax.rem(c + n, grid_cols)
 
+    def shifted(here, by, size):
+        return lax.rem(here + by, size)
+
+    other_core = r + 1 - 2 * lax.rem(r, 2)
+
+    def along_x(n):
+        x = lax.rem(c, 4)
+        return c - x + lax.rem(x + n, 4)
+
     start_copy = pltpu.make_async_copy(start_ref, start_v, start_sem)
     start_copy.start()
     block_copies = []
@@ -91,10 +103,11 @@
         block_copies.append(pltpu.make_async_copy(blocks_ref.at[part], held.at[part], block_sem.at[n]))
 
     barrier = pltpu.get_barrier_semaphore()
-    for n in range(1, grid_rows):
-        pl.semaphore_signal(barrier, inc=1, device_id=(row_peer(n), c), device_id_type=MESH)
-    for n in range(1, grid_cols):
-        pl.semaphore_signal(barrier, inc=1, device_id=(r, col_peer(n)), device_id_type=MESH)
+    near = [(other_core, c)]
+    for n in HOPS:
+        near += [(shifted(r, n * 2, grid_rows), c), (r, shifted(c, n * 4, grid_cols)), (r, along_x(n))]
+    for place in near:
+        pl.semaphore_signal(barrier, inc=1, device_id=place, device_id_type=MESH)
 
     lane = lax.broadcasted_iota(jnp.int32, (1, slots), 1)
     live = lane < count_ref[0, 0]
@@ -116,30 +129,52 @@
     image = start_v[...]
 
     def share(it, vectors):
-        copies = []
         for b in range(owned):
             rounded = vectors[:, b * side : (b + 1) * side].astype(BF16)
             row_vecs[it][c, b] = rounded
             col_vecs[it][r, b] = rounded
         if it == 0:
-            pl.semaphore_wait(barrier, grid_rows + grid_cols - 2)
-        for n in range(1, grid_rows):
-            copies.append(
-                pltpu.make_async_remote_copy(
-                    col_vecs[it].at[r], col_vecs[it].at[r], col_vec_send.at[it, n], col_vec_recv.at[it, n],
-                    device_id=(row_peer(n), c), device_id_type=MESH,
-                )
-            )
-        for n in range(1, grid_cols):
-            copies.append(
-                pltpu.make_async_remote_copy(
-                    row_vecs[it].at[c], row_vecs[it].at[c], row_vec_send.at[it, n], row_vec_recv.at[it, n],
-                    device_id=(r, col_peer(n)), device_id_type=MESH,
-                )
-            )
-        for copy in copies:
-            copy.start()
-        return copies[: grid_rows - 1], copies[grid_rows - 1 :]
+            pl.semaphore_wait(barrier, len(near))
+        sent = {}
+        for n in HOPS:
+            send_col(it, sent, 2 * n, r, shifted(r, n * 2, grid_rows))
+            send_row(it, sent, 4 * n, c, shifted(c, n * 4, grid_cols))
+            send_row(it, sent, n, c, along_x(n))
+        send_col(it, sent, 1, r, other_core)
+        return sent
+
+    def send_col(it, sent, n, source, to):
+        sent["col", n] = pltpu.make_async_remote_copy(
+            col_vecs[it].at[source], col_vecs[it].at[source], col_vec_send.at[it, n], col_vec_recv.at[it, n],
+            device_id=(to, c), device_id_type=MESH,
+        )
+        sent["col", n].start()
+
+    def send_row(it, sent, n, source, to):
+        sent["row", n] = pltpu.make_async_remote_copy(
+            row_vecs[it].at[source], row_vecs[it].at[source], row_vec_send.at[it, n], row_vec_recv.at[it, n],
+            device_id=(r, to), device_id_type=MESH,
+        )
+        sent["row", n].start()
+
+    def pass_on(it, sent):
+        for n in reversed(HOPS):
+            sent["col", 2 * n].wait_recv()
+            send_col(it, sent, 2 * n + 1, shifted(r, grid_rows - n * 2, grid_rows), other_core)
+            sent["row", 4 * n].wait_recv()
+            for m in HOPS:
+                if (n, m) in Y_FIRST:
+                    send_row(it, sent, 4 * n + m, shifted(c, grid_cols - n * 4, grid_cols), along_x(m))
+            sent["row", n].wait_recv()
+            for m in HOPS:
+                if (m, n) not in Y_FIRST:
+                    send_row(it, sent, 4 * m + n, along_x(4 - n), shifted(c, m * 4, grid_cols))
+
+    def finish(sent, axis):
+        arrived = 2 if axis == "col" else 4
+        for n in range(1, grid_rows if axis == "col" else grid_cols):
+            passed = n % arrived == 0 or (axis == "row" and n < arrived)
+            sent[axis, n].wait_send() if passed else sent[axis, n].wait()
 
     def multiply(which, matrices, vectors, it):
         def some(g, running):
@@ -208,33 +243,37 @@
     def normalise(inverse, image):
         return lax.dot_general(inverse, image, NN, precision=HIGH, preferred_element_type=F32)
 
+    def turn_chunks(first, end):
+        for n in range(first, end):
+            block_copies[n].wait()
+
+            def turn(m, _, n=n):
+                turned[n * per_chunk + m] = held[n * per_chunk + m].T
+                return 0
+
+            lax.fori_loop(0, per_chunk, turn, 0, unroll=True)
+
     for it in range(ITERS):
-        col_copies, row_copies = share(it, image)
+        sent = share(it, image)
         if it == 0:
             for copy in block_copies:
                 copy.start()
         if it > 0:
             gram_copies = gram_begin(it - 1, image)
         if it == 0:
+            turn_chunks(0, EARLY_CHUNKS)
+        pass_on(it, sent)
+        if it == 0:
+            turn_chunks(EARLY_CHUNKS, CHUNKS)
             index_copy.wait()
-            for n in range(CHUNKS):
-                block_copies[n].wait()
-
-                def turn(m, _, n=n):
-                    turned[n * per_chunk + m] = held[n * per_chunk + m].T
-                    return 0
-
-                lax.fori_loop(0, per_chunk, turn, 0, unroll=True)
-        for copy in col_copies:
-            copy.wait()
+        finish(sent, "col")
         if it > 0:
             gram_copies = gram_middle(it - 1, gram_copies)
         multiply(0, turned, col_vecs, it)
         row_moves = spread(
             it, 0, grid_cols, c, row_out, row_in, row_out_send, row_out_recv, lambda to: (r, to)
         )
-        for copy in row_copies:
-            copy.wait()
+        finish(sent, "row")
         multiply(1, held, row_vecs, it)
         col_moves = spread(
             it, 1, grid_rows, r, col_out, col_in, col_out_send, col_out_recv, lambda to: (to, c)

time: 72.1 us -> 69.7 us (0.967)
  Pallas kernels: 69.7 us -> 67.3 us
    pallas_call x1, Pallas kernels: 69.7 us -> 67.3 us  [shards(): pl.pallas_call(functools.partial(kernel, grid_rows, grid_cols, total_rows...]
where the time goes in v3:
time: 69.7 us; the launch traced here: 69.5 us
  Pallas kernels  67.3 us (97%)
  local copies, waits for them, and re-layouts  1.54 us (2%)
    pallas_call x1, Pallas kernels, shards(): pl.pallas_call(functools.partial(kernel, grid_rows, grid_cols, total_rows...  67.3 us
    unnamed x1, local copies, waits for them, and re-layouts  1.54 us

profile of v3, /device:TPU:1, one launch (start us, length us, event | category | flops | bytes accessed | tf_op | source)
XLA Modules:
  0.0 69.5 jit_solution(3940138570071858238)
XLA Ops:
  0.7 67.3 %shard_map.64 = f32[32,768]{1,0:T(8,128)} custom-call(f32[32,768]{1,0:T(8,128)} %bitcast.5, f32[768]{0:T(1024)} %weight_ref.1, bf16[128,256,256]{2,1,0:T(8,128)(2,1)} %bitcast.3, s32[1,1,128]{2,1,0:T(1,128)} %slot_row_ref.1, s32[1,1,128]{2,1,0:T(1,128)} %slot_col_ref.1, s32[1,1]{1,0:T(1,128)S(6)} %copy.8.count_ref), custom_call_target="tpu_custom_call" | custom-call | tf_op jit(solution)/shard_map/pallas_call | solution.py:322
  68.0 1.5 %copy.9 = f32[768,32]{0,1:T(8,128)} copy(f32[768,32]{0,1:T(8,128)} %bitcast.4) | data formatting | bytes 196608

commit v4 on v3

--- a/solution.py
+++ b/solution.py
@@ -14,7 +14,8 @@
 HIGH = lax.Precision.HIGHEST
 F32 = jnp.float32
 BF16 = jnp.bfloat16
-UNROLL = 32
+UNROLL = 128
+PIVOTS = 8
 HOPS = (2, 3, 1)
 Y_FIRST = ((1, 1), (1, 2), (1, 3), (2, 3), (3, 3))
 CHUNKS = 16
@@ -50,15 +51,33 @@
 
 def inverse_factor(gram):
     k = gram.shape[0]
-    row = lax.broadcasted_iota(jnp.int32, (k, 2 * k), 0)
     eye = (lax.broadcasted_iota(jnp.int32, (k, k), 0) == lax.broadcasted_iota(jnp.int32, (k, k), 1)).astype(F32)
     work = jnp.concatenate([gram, eye], axis=1)
-    for j in range(k):
-        scale = lax.rsqrt(work[j : j + 1, j : j + 1])
-        pivot = work[j : j + 1, :] * scale
-        column = work[:, j : j + 1] * scale
-        work = jnp.where(row > j, work - column * pivot, jnp.where(row == j, pivot, work))
-    return work[:, k:]
+    found = []
+    for j in range(0, k, PIVOTS):
+        rows = [work[j + n : j + n + 1, :] for n in range(PIVOTS)]
+        columns = [jnp.broadcast_to(work[:, j + n : j + n + 1], (k, 2 * k)) for n in range(PIVOTS)]
+        corner = [
+            [None] * n + [jnp.broadcast_to(rows[n][:, j + m : j + m + 1], (1, 2 * k)) for m in range(n, PIVOTS)]
+            for n in range(PIVOTS)
+        ]
+        factors, spread = {}, []
+        for n in range(PIVOTS):
+            over = 1.0 / corner[n][n]
+            for t in range(n + 1, PIVOTS):
+                factors[n, t] = corner[n][t] * over
+            for t in range(n + 1, PIVOTS):
+                rows[t] = rows[t] - factors[n, t] * rows[n]
+                for m in range(t, PIVOTS):
+                    corner[t][m] = corner[t][m] - factors[n, t] * corner[n][m]
+            spread.append(rows[n] * over)
+            found.append(rows[n][:, k:] * lax.rsqrt(corner[n][n][:, k:]))
+        for n in reversed(range(PIVOTS)):
+            for t in range(n + 1, PIVOTS):
+                spread[n] = spread[n] - factors[n, t] * spread[t]
+        for n in range(PIVOTS):
+            work = work - columns[n] * spread[n]
+    return jnp.concatenate(found, axis=0)
 
 
 def kernel(

time: 69.7 us -> 67 us (0.961)
  Pallas kernels: 67.3 us -> 64.6 us
    pallas_call x1, Pallas kernels: 67.3 us -> 64.6 us  [shards(): pl.pallas_call(functools.partial(kernel, grid_rows, grid_cols, total_rows...]
where the time goes in v4:
time: 67 us; the launch traced here: 66.8 us
  Pallas kernels  64.6 us (96%)
  local copies, waits for them, and re-layouts  1.54 us (2%)
    pallas_call x1, Pallas kernels, shards(): pl.pallas_call(functools.partial(kernel, grid_rows, grid_cols, total_rows...  64.6 us
    unnamed x1, local copies, waits for them, and re-layouts  1.54 us

profile of v4, /device:TPU:1, one launch (start us, length us, event | category | flops | bytes accessed | tf_op | source)
XLA Modules:
  0.0 66.8 jit_solution(5549355111744776504)
XLA Ops:
  0.7 64.6 %shard_map.64 = f32[32,768]{1,0:T(8,128)} custom-call(f32[32,768]{1,0:T(8,128)} %bitcast.5, f32[768]{0:T(1024)} %weight_ref.1, bf16[128,256,256]{2,1,0:T(8,128)(2,1)} %bitcast.3, s32[1,1,128]{2,1,0:T(1,128)} %slot_row_ref.1, s32[1,1,128]{2,1,0:T(1,128)} %slot_col_ref.1, s32[1,1]{1,0:T(1,128)S(6)} %copy.8.count_ref), custom_call_target="tpu_custom_call" | custom-call | tf_op jit(solution)/shard_map/pallas_call | solution.py:341
  65.2 1.5 %copy.9 = f32[768,32]{0,1:T(8,128)} copy(f32[768,32]{0,1:T(8,128)} %bitcast.4) | data formatting | bytes 196608

commit v5 on v4

--- a/solution.py
+++ b/solution.py
@@ -180,6 +180,7 @@
         for n in reversed(HOPS):
             sent["col", 2 * n].wait_recv()
             send_col(it, sent, 2 * n + 1, shifted(r, grid_rows - n * 2, grid_rows), other_core)
+        for n in reversed(HOPS):
             sent["row", 4 * n].wait_recv()
             for m in HOPS:
                 if (n, m) in Y_FIRST:
@@ -306,16 +307,14 @@
             )
         if it > 0:
             inverse = gram_end(it - 1, gram_copies)
-        for copy in col_moves:
-            copy.wait()
         for n in range(1, grid_rows):
-            at = row_peer(n)
+            col_moves[n - 1].wait()
+            at = row_peer(grid_rows - n)
             for b in range(owned):
                 parts[b] = parts[b] + col_in[it, at, b].astype(F32)
-        for copy in row_moves:
-            copy.wait()
         for n in range(1, grid_cols):
-            at = col_peer(n)
+            row_moves[n - 1].wait()
+            at = col_peer(grid_cols - n)
             for b in range(owned):
                 parts[b] = parts[b] + row_in[it, at, b].astype(F32)
         image = jnp.concatenate(parts, axis=1)

time: 67 us -> 65.9 us (0.984)
  Pallas kernels: 64.6 us -> 63.5 us
    pallas_call x1, Pallas kernels: 64.6 us -> 63.5 us  [shards(): pl.pallas_call(functools.partial(kernel, grid_rows, grid_cols, total_rows...]
where the time goes in v5:
time: 65.9 us; the launch traced here: 65.7 us
  Pallas kernels  63.5 us (96%)
  local copies, waits for them, and re-layouts  1.54 us (2%)
  between operations  0.66 us (1%)
    pallas_call x1, Pallas kernels, shards(): pl.pallas_call(functools.partial(kernel, grid_rows, grid_cols, total_rows...  63.5 us
    unnamed x1, local copies, waits for them, and re-layouts  1.54 us

profile of v5, /device:TPU:1, one launch (start us, length us, event | category | flops | bytes accessed | tf_op | source)
XLA Modules:
  0.0 65.7 jit_solution(2184013970139177914)
XLA Ops:
  0.7 63.5 %shard_map.64 = f32[32,768]{1,0:T(8,128)} custom-call(f32[32,768]{1,0:T(8,128)} %bitcast.5, f32[768]{0:T(1024)} %weight_ref.1, bf16[128,256,256]{2,1,0:T(8,128)(2,1)} %bitcast.3, s32[1,1,128]{2,1,0:T(1,128)} %slot_row_ref.1, s32[1,1,128]{2,1,0:T(1,128)} %slot_col_ref.1, s32[1,1]{1,0:T(1,128)S(6)} %copy.8.count_ref), custom_call_target="tpu_custom_call" | custom-call | tf_op jit(solution)/shard_map/pallas_call | solution.py:340
  64.1 1.5 %copy.9 = f32[768,32]{0,1:T(8,128)} copy(f32[768,32]{0,1:T(8,128)} %bitcast.4) | data formatting | bytes 196608
